TPU v7x, 32 devices: a whole 2x2x4 slice. The times are simulated.
32 devices in a mesh: row: 4 (over z), col: 8 (over y, x, core).
Axes of the slice: x: 2, y: 2, z: 4, core: 2. Of those that a mesh axis runs over, the one named last changes fastest.
Arguments:
- momentum: float32 [8192, 28672], P('row', 'col'), may hold values from -400 to 400, as said below
- gradient: bfloat16 [8192, 28672], P('row', 'col'), may hold values from -3 to 3
- right_prev: float32 [28672, 256], P('col'), may hold values from -5 to 5
Outputs:
- new_momentum: float32 [8192, 28672], P('row', 'col')
- right_next: float32 [28672, 256], P('col')
- update: bfloat16 [8192, 28672], P('row', 'col')
Inputs may be any that keep to these rules, and one draw needn't show every extreme that they name: momentum entries are finite reals.
All inputs are finite; a program needn't handle non-finite values.
Results may differ from a plain program's by a relative error of at most 0.001.
Values sent between devices are 32-bit elements; how exact they have to be, the bound alone decides.
A program may use at most 192 MiB of HBM per device.

v0:
```python
import jax
import jax.numpy as jnp
from jax import lax
from jax.sharding import PartitionSpec as P

D = 8192
FF = 28672
RANK = 256


HI = lax.Precision.HIGHEST


def orthogonal(left, gram):
    chol = jnp.linalg.cholesky(gram)
    return jax.scipy.linalg.solve_triangular(chol, left.T, lower=True).T


def on_device(momentum, gradient, right_prev):
    merged = momentum + gradient.astype(jnp.float32)
    partial_value = jnp.dot(merged, right_prev, precision=HI, preferred_element_type=jnp.float32)
    left = lax.psum(partial_value, "col")
    gram = lax.psum(jnp.dot(left.T, left, precision=HI, preferred_element_type=jnp.float32), "row")
    ortho = orthogonal(left, gram)
    right_part = lax.psum_scatter(
        jnp.dot(merged.T, ortho, precision=HI, preferred_element_type=jnp.float32),
        "row",
        scatter_dimension=0,
        tiled=True,
    )
    colsq = lax.psum(jnp.sum(right_part * right_part, axis=0), ("row", "col"))
    right = lax.all_gather(right_part, "row", axis=0, tiled=True)
    right_next = right * lax.rsqrt(colsq / FF + 1e-06)
    new_momentum = merged - 0.05 * jnp.dot(
        ortho, right.T, precision=HI, preferred_element_type=jnp.float32
    )
    factor = jnp.sqrt(jnp.float32(D) / jnp.float32(RANK))
    update = (
        factor * jnp.dot(ortho, right_next.T, precision=HI, preferred_element_type=jnp.float32)
    ).astype(jnp.bfloat16)
    return (new_momentum, right_next, update)


def solution(mesh):
    in_specs = (P("row", "col"), P("row", "col"), P("col", None))
    out_specs = (P("row", "col"), P("col", None), P("row", "col"))
    return jax.shard_map(
        on_device, mesh=mesh, in_specs=in_specs, out_specs=out_specs, check_vma=False
    )
```

profile of v0, /device:TPU:0, one launch (start us, length us, event | category | flops | bytes accessed | tf_op | source)
XLA Modules:
  0.0 517.4 jit_solution(5718696614336531558)
XLA Ops:
  7.2 0.0 all-reduce.4.cloned.1.call-start
  7.2 30.6 %fusion.1 = f32[2048,256]{1,0:T(8,128)} fusion(f32[3584,256]{1,0:T(8,128)} %param.5, f32[2048,3584]{1,0:T(8,128)} %param.3, bf16[2048,3584]{1,0:T(8,128)(2,1)} %param.4), kind=kOutput, calls=%fused_computation.6 | convolution fusion | flops 22563258368 | bytes 49807360 | tf_op jit(solution)/shard_map/dot_general | solution.py:21
  37.8 0.0 all-reduce.4.cloned.1.call-update
  37.8 0.0 all-reduce.6.cloned.1.call-start
  37.9 64.2 %all-reduce.4.cloned.1.call-done = f32[2048,256]{1,0:T(8,128)} async-done(((f32[2048,256]{1,0:T(8,128)}), f32[2048,256]{1,0:T(8,128)}) %all-reduce.4.cloned.1.call-update) | async-done | bytes 2097168 | tf_op jit(solution)/shard_map/psum | solution.py:22
  102.1 0.0 copy-start
  102.1 6.5 %fusion.14 = f32[256,256]{0,1:T(8,128)} fusion(f32[2048,256]{1,0:T(8,128)} %all-reduce.4.cloned.1.call-done), kind=kOutput, calls=%fused_computation.40 | convolution fusion | flops 1610612736 | bytes 2359296 | tf_op jit(solution)/shard_map/dot_general | solution.py:23
  108.6 0.0 all-reduce.6.cloned.1.call-update
  108.6 0.2 reduce-scatter.2.cloned.1.call-start
  108.9 34.4 %all-reduce.6.cloned.1.call-done = f32[256,256]{0,1:T(8,128)} async-done(((f32[256,256]{0,1:T(8,128)}), f32[256,256]{0,1:T(8,128)}) %all-reduce.6.cloned.1.call-update) | async-done | bytes 262160 | tf_op jit(solution)/shard_map/psum | solution.py:23
  143.3 1.1 copy.7
  144.4 1.0 fusion.4
  145.4 11.7 %cholesky.50 = f32[128,128]{1,0:T(8,128)S(1)} custom-call(f32[128,128]{1,0:T(8,128)S(1)} %cholesky.118), custom_call_target="Cholesky" | custom-call | tf_op jit(solution)/shard_map/jit(cholesky)/cholesky | solution.py:15
  157.2 9.8 %custom-call.15 = f32[1,128,128]{1,2,0:T(8,128)S(1)} custom-call(f32[1,128,128]{2,1,0:T(8,128)S(1)} %get-tuple-element.24), custom_call_target="InvertDiagBlocksLowerTriangular" | custom-call | tf_op jit(solution)/shard_map/jit(cholesky)/cholesky | solution.py:15
  167.0 0.2 constant_dynamic-update-slice_fusion.1
  167.2 0.3 convolution_subtract_fusion.1
  167.4 11.7 %cholesky.105 = f32[128,128]{1,0:T(8,128)S(1)} custom-call(f32[128,128]{1,0:T(8,128)S(1)} %convolution_subtract_fusion.1), custom_call_target="Cholesky" | custom-call | tf_op jit(solution)/shard_map/jit(cholesky)/cholesky | solution.py:15
  179.2 0.6 compare_reduce_fusion
  181.2 0.1 triangular_solve.57
  181.3 4.0 while.1
  181.3 0.6 fusion.25
  181.8 1.4 bitcast_dynamic-update-slice_fusion.2
  183.3 0.6 fusion.25
  183.8 1.4 bitcast_dynamic-update-slice_fusion.2
  185.2 19.7 %custom-call.16 = f32[2,128,128]{1,2,0:T(8,128)S(1)} custom-call(f32[2,128,128]{2,1,0:T(8,128)S(1)} %get-tuple-element.10), custom_call_target="InvertDiagBlocksLowerTriangular" | custom-call | tf_op jit(solution)/shard_map/jit(_solve_triangular)/triangular_solve | solution.py:16
  204.9 0.0 copy-done
  204.9 1.1 fusion.2
  206.0 1.8 convolution_subtract_fusion
  207.8 1.1 fusion.6
  208.9 51.8 %fusion = f32[3584,256]{1,0:T(8,128)} fusion(f32[2048,3584]{1,0:T(8,128)} %param.3, bf16[2048,3584]{1,0:T(8,128)(2,1)} %param.4, f32[128,2048]{1,0:T(8,128)S(1)} %fusion.6, f32[128,2048]{1,0:T(8,128)S(1)} %fusion.2), kind=kOutput, calls=%fused_computation.5 | convolution fusion | flops 22563782656 | bytes 49807360 | tf_op jit(solution)/shard_map/dot_general | solution.py:26
  260.7 0.0 reduce-scatter.2.cloned.1.call-update
  260.7 0.0 all-gather.2.cloned.1.call-start
  260.8 68.2 %reduce-scatter.2.cloned.1.call-done = f32[896,256]{1,0:T(8,128)} async-done(((f32[3584,256]{1,0:T(8,128)}), f32[896,256]{1,0:T(8,128)}) %reduce-scatter.2.cloned.1.call-update) | async-done | bytes 917520 | tf_op jit(solution)/shard_map/reduce_scatter | solution.py:25
  329.0 0.0 all-gather.2.cloned.1.call-update
  329.0 1.3 multiply_reduce_fusion
  330.4 44.2 %psum.23 = f32[256]{0:T(256)S(1)} all-reduce(f32[256]{0:T(256)S(1)} %multiply_reduce_fusion), channel_id=1, replica_groups=mesh['row'=4,'col'=8] {'row','col'}, use_global_device_ids=true, to_apply=%region_8.9 | all-reduce | flops 256 | bytes 2048 | tf_op jit(solution)/shard_map/psum | solution.py:31
  374.6 29.4 %all-gather.2.cloned.1.call-done = f32[3584,256]{1,0:T(8,128)} async-done(((f32[896,256]{1,0:T(8,128)}), f32[3584,256]{1,0:T(8,128)}) %all-gather.2.cloned.1.call-update) | async-done | bytes 3670032 | tf_op jit(solution)/shard_map/all_gather | solution.py:32
  404.0 2.3 broadcast_multiply_fusion
  406.3 0.0 copy-start.1
  406.3 48.5 %multiply_convert_fusion = bf16[2048,3584]{1,0:T(8,128)(2,1)} fusion(f32[3584,256]{1,0:T(8,128)S(1)} %broadcast_multiply_fusion, f32[128,2048]{1,0:T(8,128)S(1)} %fusion.6, f32[128,2048]{1,0:T(8,128)S(1)} %fusion.2), kind=kOutput, calls=%fused_computation.2 | convolution fusion | flops 22563782656 | bytes 20447232 | tf_op jit(solution)/shard_map/dot_general | solution.py:39
  454.8 0.0 copy-done.1
  454.9 55.8 %multiply_subtract_fusion = f32[2048,3584]{1,0:T(8,128)} fusion(f32[3584,256]{1,0:T(8,128)} %all-gather.2.cloned.1.call-done, f32[2048,3584]{1,0:T(8,128)} %param.3, bf16[2048,3584]{1,0:T(8,128)(2,1)} %param.4, f32[128,2048]{1,0:T(8,128)S(1)} %fusion.6, f32[128,2048]{1,0:T(8,128)S(1)} %fusion.2), kind=kOutput, calls=%fused_computation.3 | convolution fusion | flops 22578462720 | bytes 79167488 | tf_op jit(solution)/shard_map/dot_general | solution.py:34
  (10 shorter events, 0.2 us)
Async XLA Ops:
  7.2 94.9 %all-reduce.4.cloned.1.call-start = ((), (), s32[]{:S(2)}) async-start(), calls=%async_computation.1 | async-start | bytes 4194304 | tf_op jit(solution)/shard_map/psum | solution.py:22
  37.8 105.5 %all-reduce.6.cloned.1.call-start = ((), (), s32[]{:S(2)}) async-start(), calls=%async_computation.2 | async-start | bytes 524288 | tf_op jit(solution)/shard_map/psum | solution.py:23
  102.1 102.8 %copy-start = (f32[2048,256]{1,0:T(8,128)S(1)}, f32[2048,256]{1,0:T(8,128)}, u32[]{:S(2)}) copy-start(f32[2048,256]{1,0:T(8,128)} %all-reduce.4.cloned.1.call-done) | copy-start | bytes 6291460
  108.6 220.4 %reduce-scatter.2.cloned.1.call-start = ((), (), s32[]{:S(2)}) async-start(), calls=%async_computation.3 | async-start | bytes 4587520 | tf_op jit(solution)/shard_map/reduce_scatter | solution.py:25
  260.7 143.3 %all-gather.2.cloned.1.call-start = ((), (), s32[]{:S(2)}) async-start(), calls=%async_computation.4 | async-start | bytes 4587520 | tf_op jit(solution)/shard_map/all_gather | solution.py:32
  406.3 48.5 %copy-start.1 = (f32[3584,256]{1,0:T(8,128)}, f32[3584,256]{1,0:T(8,128)S(1)}, u32[]{:S(2)}) copy-start(f32[3584,256]{1,0:T(8,128)S(1)} %broadcast_multiply_fusion) | copy-start | bytes 11010052
Sparse Core Ops, SparseCore 0:
  38.0 64.0 all-reduce.3
  108.8 34.4 all-reduce.5
  260.8 68.1 reduce-scatter.1
  330.5 73.4 all-gather.1
where the time goes:
time: 525 us; the launch traced here: 517 us
  matrix products  198 us (38%)
  waiting for transfers between devices  196 us (37%)
  other arithmetic  58.2 us (11%)
  blocking collectives  44.2 us (8%)
  between operations  15.4 us (3%)
    reduce_scatter x1, waiting for transfers between devices, on_device(): lax.psum_scatter(jnp.dot(merged.T, ortho, precision=HI, preferred_element...  68.2 us
    psum x1, waiting for transfers between devices, on_device(): left = lax.psum(partial_value, 'col')  64.2 us
    dot_general x1, matrix products, on_device(): jnp.dot(ortho, right.T, precision=HI, preferred_element_type=jnp.float32)  55.8 us
    dot_general x1, matrix products, on_device(): jnp.dot(merged.T, ortho, precision=HI, preferred_element_type=jnp.float32)  51.8 us
    dot_general x1, matrix products, on_device(): jnp.dot(ortho, right_next.T, precision=HI, preferred_element_type=jnp.flo...  48.5 us
    psum x1, blocking collectives, on_device(): colsq = lax.psum(jnp.sum(right_part * right_part, axis=0), ('row', 'col'))  44.2 us
    psum x1, waiting for transfers between devices, on_device(): lax.psum(jnp.dot(left.T, left, precision=HI, preferred_element_type=jnp.f...  34.4 us
    another operation x6, other arithmetic, orthogonal(): chol = jnp.linalg.cholesky(gram)  33.9 us
  transfers between devices with their start and end apart: 4, of which 4 were waited for; matrix products, arithmetic and copies ran while one was open for 0% of the time, Pallas kernels for 0%

commit v1 on v0

v1 whole, which is shorter than its diff:
```python
import functools
import jax
import jax.numpy as jnp
from jax import lax
from jax.experimental import pallas as pl
from jax.experimental.pallas import tpu as pltpu
from jax.sharding import PartitionSpec as P

HI = lax.Precision.HIGHEST
MESH = pl.DeviceIdType.MESH
F32, BF16 = jnp.float32, jnp.bfloat16
CHUNK = 128
PANEL = 16


def rcopy(src, dst, ssem, rsem, device):
    return pltpu.make_async_remote_copy(
        src_ref=src, dst_ref=dst, send_sem=ssem, recv_sem=rsem, device_id=device, device_id_type=MESH
    )


def signal(sem, device):
    pl.semaphore_signal(sem, inc=1, device_id=device, device_id_type=MESH)


def left_sum(chips, x_ref, o_ref, got, acc, sums, full, s1, r1, s2, r2, s3, r3, s4, r4):
    me = lax.axis_index("col")
    core, chip = lax.rem(me, 2), me // 2
    sib = {"col": me + 1 - 2 * core}
    barrier = pltpu.get_barrier_semaphore()
    signal(barrier, sib)
    for k in range(1, chips):
        signal(barrier, {"col": 2 * lax.rem(chip + k, chips) + core})
    pl.semaphore_wait(barrier, chips)

    def pair(k):
        q = lax.rem(chip + k, chips)
        return rcopy(x_ref.at[q, 1 - core], got.at[k], s1.at[k], r1.at[k], sib)

    def scatter(k):
        q = lax.rem(chip + k, chips)
        return rcopy(acc.at[k], sums.at[k - 1], s2.at[k - 1], r2.at[k - 1], {"col": 2 * q + core})

    order = list(range(chips // 2, chips)) + list(range(1, chips // 2)) + [0] if chips > 1 else [0]
    for k in order:
        pair(k).start()
    for k in order:
        pair(k).wait_recv()
        q = lax.rem(chip + k, chips)
        acc[k] = x_ref[q, core] + got[k]
        if k:
            scatter(k).start()
    total = acc[0]
    for k in [k for k in order if k]:
        scatter(k).wait_recv()
        total = total + sums[k - 1]
    full[chip, core] = total

    def gather(k):
        q = lax.rem(chip + k, chips)
        return rcopy(
            full.at[chip, core], full.at[chip, core], s3.at[k - 1], r3.at[k - 1], {"col": 2 * q + core}
        )

    def forward(k):
        q = lax.rem(chip - k + chips, chips)
        return rcopy(full.at[q, core], full.at[q, core], s4.at[k], r4.at[k], sib)

    for k in [k for k in order if k]:
        gather(k).start()
    forward(0).start()
    for k in [k for k in order if k]:
        q = lax.rem(chip - k + chips, chips)
        rcopy(
            full.at[q, core], full.at[q, core], s3.at[k - 1], r3.at[k - 1], {"col": 2 * q + core}
        ).wait_recv()
        forward(k).start()
    for k in range(chips):
        q = lax.rem(chip - k + chips, chips)
        rcopy(full.at[q, 1 - core], full.at[q, 1 - core], s4.at[k], r4.at[k], sib).wait_recv()
    for k in range(chips):
        pair(k).wait_send()
        forward(k).wait_send()
        if k:
            scatter(k).wait_send()
            gather(k).wait_send()
    o_ref[...] = full[...]


def all_reduce_left(part, n):
    rows, rank = part.shape
    chips, s = n // 2, rows // n
    dma = pltpu.SemaphoreType.DMA
    out = pl.pallas_call(
        functools.partial(left_sum, chips),
        out_shape=jax.ShapeDtypeStruct((chips, 2, s, rank), F32),
        in_specs=[pl.BlockSpec(memory_space=pltpu.VMEM)],
        out_specs=pl.BlockSpec(memory_space=pltpu.VMEM),
        scratch_shapes=[
            pltpu.VMEM((chips, s, rank), F32),
            pltpu.VMEM((chips, s, rank), F32),
            pltpu.VMEM((max(chips - 1, 1), s, rank), F32),
            pltpu.VMEM((chips, 2, s, rank), F32),
            dma((chips,)), dma((chips,)),
            dma((max(chips - 1, 1),)), dma((max(chips - 1, 1),)),
            dma((max(chips - 1, 1),)), dma((max(chips - 1, 1),)),
            dma((chips,)), dma((chips,)),
        ],
        compiler_params=pltpu.CompilerParams(
            collective_id=0, has_side_effects=True, vmem_limit_bytes=32 * 2**20
        ),
        name="left_sum",
    )(part.reshape(chips, 2, s, rank))
    return out.reshape(rows, rank)


def panel_step(mat, p):
    rank, wide = mat.shape
    first = p * PANEL
    rows0 = pl.ds(pl.multiple_of(first, PANEL), PANEL)
    sub = lax.broadcasted_iota(jnp.int32, (PANEL, wide), 0)
    lane = lax.broadcasted_iota(jnp.int32, (PANEL, wide), 1)

    def step(k, block):
        col = jnp.sum(jnp.where(lane == first + k, block, 0.0), axis=1, keepdims=True)
        row = jnp.sum(jnp.where(sub == k, block, 0.0), axis=0, keepdims=True)
        pivot = jnp.sum(jnp.where(sub[:, :1] == k, col, 0.0), axis=0, keepdims=True)
        inv = lax.rsqrt(pivot)
        inv = inv * (1.5 - 0.5 * (pivot * inv) * inv)
        u = row * inv
        factor = jnp.where(sub[:, :1] > k, col * inv, 0.0)
        return jnp.where(sub == k, u, block - factor * u)

    u = lax.fori_loop(0, PANEL, step, mat[rows0, :])
    mat[rows0, :] = u
    drop = lax.dot_general(
        u[:, :rank], u, (((0,), (0,)), ((), ())), precision=HI, preferred_element_type=F32
    )
    below = lax.broadcasted_iota(jnp.int32, (rank, wide), 0) >= first + PANEL
    mat[...] = jnp.where(below, mat[...] - drop, mat[...])


def times_inverse(a, inverse):
    return lax.dot_general(
        a, inverse, (((1,), (1,)), ((), ())), precision=HI, preferred_element_type=F32
    )


def split(a):
    hi = a.astype(BF16)
    return hi, (a - hi.astype(F32)).astype(BF16)


def right_sum(
    n, cols, ff, gram_ref, w_ref, left_ref,
    next_ref, nh_ref, nl_ref, rb_ref, oh_ref, ol_ref,
    x, outer_in, inner_in, mat, colsq, s_in, r_outer, s_out, r_inner, s_c, r_c,
):
    me, mc = lax.axis_index("row"), lax.axis_index("col")
    half = n // 2
    low = me < half
    depth = jnp.where(low, half - 1 - me, me - half)
    inward = {"row": jnp.where(low, me + 1, me - 1)}
    has_outer = depth < half - 1
    outward = {"row": jnp.where(has_outer, jnp.where(low, me - 1, me + 1), me)}
    rank = gram_ref.shape[0]
    ffl = w_ref.shape[0]
    chunks = (rank + ffl) // CHUNK
    gram_chunks, panels = rank // CHUNK, rank // PANEL

    barrier = pltpu.get_barrier_semaphore()
    for k in range(1, cols):
        signal(barrier, {"col": lax.rem(mc + k, cols)})
    signal(barrier, inward)

    @pl.when(has_outer)
    def _():
        signal(barrier, outward)

    @pl.when(has_outer)
    def _():
        pl.semaphore_wait(barrier, cols + 1)

    @pl.when(jnp.logical_not(has_outer))
    def _():
        pl.semaphore_wait(barrier, cols)

    x[pl.ds(0, rank), :] = gram_ref[...]
    x[pl.ds(rank, ffl), :] = w_ref[...]

    def at(c):
        return pl.ds(pl.multiple_of(c * CHUNK, CHUNK), CHUNK)

    def to_inner(c):
        return rcopy(x.at[at(c)], outer_in.at[at(c)], s_in.at[c], r_outer.at[c], inward)

    def to_partner(c):
        return rcopy(x.at[at(c)], inner_in.at[at(c)], s_in.at[c], r_inner.at[c], inward)

    def to_outer(c):
        return rcopy(outer_in.at[at(c)], inner_in.at[at(c)], s_out.at[c], r_inner.at[c], outward)

    lag = 2 + 3 * depth

    def turn(t, carry):
        @pl.when(t < chunks)
        def _():
            @pl.when(has_outer)
            def _():
                to_inner(t).wait_recv()
                x[at(t), :] = x[at(t), :] + outer_in[at(t), :]

            @pl.when(depth > 0)
            def _():
                to_inner(t).start()

            @pl.when(depth == 0)
            def _():
                to_partner(t).start()

        c = t - lag

        @pl.when((c >= 0) & (c < chunks))
        def _():
            to_partner(c).wait_recv()

            @pl.when(depth == 0)
            def _():
                outer_in[at(c), :] = x[at(c), :] + inner_in[at(c), :]

            @pl.when(depth > 0)
            def _():
                outer_in[at(c), :] = inner_in[at(c), :]

            @pl.when(has_outer)
            def _():
                to_outer(c).start()

        @pl.when(c == gram_chunks - 1)
        def _():
            mat[:, pl.ds(0, rank)] = outer_in[pl.ds(0, rank), :]
            i0 = lax.broadcasted_iota(jnp.int32, (rank, rank), 0)
            i1 = lax.broadcasted_iota(jnp.int32, (rank, rank), 1)
            mat[:, pl.ds(rank, rank)] = jnp.where(i0 == i1, 1.0, 0.0).astype(F32)

        @pl.when((c >= gram_chunks) & (c < gram_chunks + panels))
        def _():
            panel_step(mat, c - gram_chunks)

        return carry

    turns = max(chunks, gram_chunks + panels) + 2 + 3 * (half - 1)
    lax.fori_loop(0, turns, turn, 0)

    inverse = mat[:, pl.ds(rank, rank)]

    def to_right(b, total):
        here = pl.ds(pl.multiple_of(b * CHUNK, CHUNK), CHUNK)
        there = pl.ds(pl.multiple_of(rank + b * CHUNK, CHUNK), CHUNK)
        value = times_inverse(outer_in[there, :], inverse)
        next_ref[here, :] = value
        rb_ref[here, :] = (0.05 * value).astype(BF16)
        return total + jnp.sum(value * value, axis=0, keepdims=True)

    part = lax.fori_loop(0, ffl // CHUNK, to_right, jnp.zeros((1, rank), F32))
    colsq[mc] = jnp.broadcast_to(part, (8, rank))

    def share(k):
        return rcopy(
            colsq.at[mc], colsq.at[mc], s_c.at[k - 1], r_c.at[k - 1], {"col": lax.rem(mc + k, cols)}
        )

    for k in range(1, cols):
        share(k).start()

    def to_ortho(b, carry):
        here = pl.ds(pl.multiple_of(b * CHUNK, CHUNK), CHUNK)
        hi, lo = split(times_inverse(left_ref[here, :], inverse))
        oh_ref[here, :] = hi
        ol_ref[here, :] = lo
        return carry

    lax.fori_loop(0, left_ref.shape[0] // CHUNK, to_ortho, 0)

    for k in range(1, cols):
        q = lax.rem(mc - k + cols, cols)
        rcopy(colsq.at[q], colsq.at[q], s_c.at[k - 1], r_c.at[k - 1], {"col": q}).wait_recv()
    total = colsq[0]
    for q in range(1, cols):
        total = total + colsq[q]
    scale = 1.0 / jnp.sqrt(total[:1] / ff + 1e-6)

    def to_next(b, carry):
        here = pl.ds(pl.multiple_of(b * CHUNK, CHUNK), CHUNK)
        value = next_ref[here, :] * scale
        next_ref[here, :] = value
        hi, lo = split(value)
        nh_ref[here, :] = hi
        nl_ref[here, :] = lo
        return carry

    lax.fori_loop(0, ffl // CHUNK, to_next, 0)

    def drain(c, carry):
        to_inner(c).wait_send()

        @pl.when(has_outer)
        def _():
            to_outer(c).wait_send()

        return carry

    lax.fori_loop(0, chunks, drain, 0)
    for k in range(1, cols):
        share(k).wait_send()


def right_factor(gram, w, left, n, cols, ff):
    rank, ffl, rows = gram.shape[0], w.shape[0], left.shape[0]
    chunks = (rank + ffl) // CHUNK
    dma = pltpu.SemaphoreType.DMA
    vm = pl.BlockSpec(memory_space=pltpu.VMEM)
    return pl.pallas_call(
        functools.partial(right_sum, n, cols, float(ff)),
        out_shape=[
            jax.ShapeDtypeStruct((ffl, rank), F32),
            jax.ShapeDtypeStruct((ffl, rank), BF16),
            jax.ShapeDtypeStruct((ffl, rank), BF16),
            jax.ShapeDtypeStruct((ffl, rank), BF16),
            jax.ShapeDtypeStruct((rows, rank), BF16),
            jax.ShapeDtypeStruct((rows, rank), BF16),
        ],
        in_specs=[vm] * 3,
        out_specs=[vm] * 6,
        scratch_shapes=[
            pltpu.VMEM((rank + ffl, rank), F32),
            pltpu.VMEM((rank + ffl, rank), F32),
            pltpu.VMEM((rank + ffl, rank), F32),
            pltpu.VMEM((rank, 2 * rank), F32),
            pltpu.VMEM((cols, 8, rank), F32),
            dma((chunks,)), dma((chunks,)), dma((chunks,)), dma((chunks,)),
            dma((cols - 1,)), dma((cols - 1,)),
        ],
        compiler_params=pltpu.CompilerParams(
            collective_id=1, has_side_effects=True, vmem_limit_bytes=48 * 2**20
        ),
        name="right_sum",
    )(gram, w, left)


def finish(factor, m_ref, g_ref, oh_ref, ol_ref, nh_ref, nl_ref, rb_ref, new_ref, up_ref):
    def nt(a, b):
        return lax.dot_general(a, b, (((1,), (1,)), ((), ())), preferred_element_type=F32)

    oh = oh_ref[...]
    new_ref[...] = (m_ref[...] + g_ref[...].astype(F32)) - nt(oh, rb_ref[...])
    up = nt(oh, nh_ref[...]) + (nt(oh, nl_ref[...]) + nt(ol_ref[...], nh_ref[...]))
    up_ref[...] = (factor * up).astype(BF16)


def divisor(size, most):
    return max(t for t in range(128, most + 1, 128) if size % t == 0)


def outputs(m, g, oh, ol, nh, nl, rb, factor):
    rows, cols = m.shape
    rank = oh.shape[1]
    tm, tn = divisor(rows, 256), divisor(cols, 1792)
    tile = pl.BlockSpec((tm, tn), lambda j, i: (i, j))
    o = pl.BlockSpec((tm, rank), lambda j, i: (i, 0))
    r = pl.BlockSpec((tn, rank), lambda j, i: (j, 0))
    return pl.pallas_call(
        functools.partial(finish, factor),
        grid=(cols // tn, rows // tm),
        out_shape=[jax.ShapeDtypeStruct((rows, cols), F32), jax.ShapeDtypeStruct((rows, cols), BF16)],
        in_specs=[tile, tile, o, o, r, r, r],
        out_specs=[tile, tile],
        compiler_params=pltpu.CompilerParams(vmem_limit_bytes=48 * 2**20),
        name="finish",
    )(m, g, oh, ol, nh, nl, rb)


def solution(mesh):
    n, cols = mesh.shape["row"], mesh.shape["col"]

    def on_device(momentum, gradient, right_prev):
        ff, rank = right_prev.shape[0] * cols, right_prev.shape[1]
        d = momentum.shape[0] * n
        merged = momentum + gradient.astype(F32)
        part = jnp.dot(merged, right_prev, precision=lax.Precision.HIGH, preferred_element_type=F32)
        left = all_reduce_left(part, cols)
        gram = jnp.dot(left.T, left, precision=HI, preferred_element_type=F32)
        w = jnp.dot(merged.T, left, precision=lax.Precision.HIGH, preferred_element_type=F32)
        right_next, nh, nl, rb, oh, ol = right_factor(gram, w, left, n, cols, ff)
        new_momentum, update = outputs(
            momentum, gradient, oh, ol, nh, nl, rb, (d / rank) ** 0.5
        )
        return new_momentum, right_next, update

    in_specs = (P("row", "col"), P("row", "col"), P("col", None))
    out_specs = (P("row", "col"), P("col", None), P("row", "col"))
    return jax.shard_map(
        on_device, mesh=mesh, in_specs=in_specs, out_specs=out_specs, check_vma=False
    )
```

time: 525 us -> 256 us (0.49); the launches traced: 517 us -> 255 us
  Pallas kernels: 0 us -> 199 us
  waiting for transfers between devices: 196 us -> 0 us
  matrix products: 198 us -> 53.5 us
  other arithmetic: 58.2 us -> 0 us
  blocking collectives: 44.2 us -> 0 us
  between operations: 15.4 us -> 0.68 us
    pallas_call x0 -> x3, Pallas kernels: none -> 199 us  [the longest x1 127 us: right_factor(): pl.pallas_call(functools.partial(right_sum, n, cols, float(ff)), out_shap...]
    dot_general x5 -> x3, matrix products: 193 us -> 53.5 us  [the longest x1 29.9 us: on_device(): jnp.dot(merged.T, left, precision=lax.Precision.HIGH, preferred_element_t...]
    psum x2 -> x0, waiting for transfers between devices: 98.6 us -> none  [the longest x1 64.2 us: on_device(): left = lax.psum(partial_value, 'col')]
    reduce_scatter x1 -> x0, waiting for transfers between devices: 68.2 us -> none  [on_device(): lax.psum_scatter(jnp.dot(merged.T, ortho, precision=HI, preferred_element...]
    another operation x9 -> x0, other arithmetic: 53.7 us -> none  [the longest x6 33.9 us: orthogonal(): chol = jnp.linalg.cholesky(gram)]
    psum x1 -> x0, blocking collectives: 44.2 us -> none  [on_device(): colsq = lax.psum(jnp.sum(right_part * right_part, axis=0), ('row', 'col'))]
    all_gather x1 -> x0, waiting for transfers between devices: 29.4 us -> none  [on_device(): right = lax.all_gather(right_part, 'row', axis=0, tiled=True)]
  transfers between devices with their start and end apart: 4 -> 0, of which waited for: 4 -> 0; matrix products, arithmetic and copies ran while one was open for 0% -> 0% of each run, Pallas kernels for 0% -> 0%
where the time goes in v1:
time: 256 us; the launch traced here: 255 us
  Pallas kernels  199 us (78%)
  matrix products  53.5 us (21%)
    pallas_call x1, Pallas kernels, right_factor(): pl.pallas_call(functools.partial(right_sum, n, cols, float(ff)), out_shap...  127 us
    pallas_call x1, Pallas kernels, outputs(): pl.pallas_call(functools.partial(finish, factor), grid=(cols // tn, rows...  39 us
    pallas_call x1, Pallas kernels, all_reduce_left(): pl.pallas_call(functools.partial(left_sum, chips), out_shape=jax.ShapeDty...  33.3 us
    dot_general x1, matrix products, on_device(): jnp.dot(merged.T, left, precision=lax.Precision.HIGH, preferred_element_t...  29.9 us
    dot_general x1, matrix products, on_device(): jnp.dot(merged, right_prev, precision=lax.Precision.HIGH, preferred_eleme...  20 us

profile of v1, /device:TPU:0, one launch (start us, length us, event | category | flops | bytes accessed | tf_op | source)
XLA Modules:
  0.0 255.2 jit_solution(9869790819642461245)
XLA Ops:
  0.6 20.0 %fusion.1 = f32[2048,256]{1,0:T(8,128)S(1)} fusion(f32[3584,256]{1,0:T(8,128)} %param.5, f32[2048,3584]{1,0:T(8,128)} %m_ref.1, bf16[2048,3584]{1,0:T(8,128)(2,1)} %g_ref.1), kind=kOutput, calls=%fused_computation.2 | convolution fusion | flops 11288969216 | bytes 49807360 | tf_op jit(solution)/shard_map/dot_general | solution.py:390
  20.6 33.3 %left_sum.1 = f32[4,2,256,256]{3,2,1,0:T(8,128)S(1)} custom-call(f32[4,2,256,256]{3,2,1,0:T(8,128)S(1)} %bitcast.12), custom_call_target="tpu_custom_call" | custom-call | tf_op jit(solution)/shard_map/left_sum/pallas_call | solution.py:94
  53.9 0.0 copy-start
  53.9 3.6 %convolution_bitcast_fusion.gram_ref = f32[256,256]{1,0:T(8,128)S(1)} fusion(f32[4,2,256,256]{3,2,1,0:T(8,128)S(1)} %left_sum.1), kind=kOutput, calls=%fused_computation.3 | convolution fusion | flops 1610612736 | bytes 2359296 | tf_op jit(solution)/shard_map/dot_general | solution.py:392
  57.6 29.9 %fusion.w_ref = f32[3584,256]{1,0:T(8,128)} fusion(f32[2048,256]{1,0:T(8,128)S(1)} %bitcast.10, f32[2048,3584]{1,0:T(8,128)} %m_ref.1, bf16[2048,3584]{1,0:T(8,128)(2,1)} %g_ref.1), kind=kOutput, calls=%fused_computation.1 | convolution fusion | flops 11288969216 | bytes 49807360 | tf_op jit(solution)/shard_map/dot_general | solution.py:393
  87.5 0.0 copy-done
  87.5 126.9 %right_sum.1 = (f32[3584,256]{1,0:T(8,128)}, bf16[3584,256]{1,0:T(8,128)(2,1)S(1)}, bf16[3584,256]{1,0:T(8,128)(2,1)S(1)}, bf16[3584,256]{1,0:T(8,128)(2,1)}, bf...) custom-call(f32[256,256]{1,0:T(8,128)S(1)} %convolution_bitcast_fusion.gram_ref, f32[3584,256]{1,0:T(8,128)} %fusion.w_ref, ...), custom_call_target="tpu_custom_call" | custom-call | tf_op jit(solution)/shard_map/right_sum/pallas_call | solution.py:323
  214.4 0.0 copy-start.1
  214.4 39.0 %finish.1 = (f32[2048,3584]{1,0:T(8,128)}, bf16[2048,3584]{1,0:T(8,128)(2,1)}) custom-call(f32[2048,3584]{1,0:T(8,128)} %m_ref.1, bf16[2048,3584]{1,0:T(8,128)(2,1)} %g_ref.1, bf16[2048,256]{1,0:T(8,128)(2,1)S(1)} %get-tuple-element.11.oh_ref, bf16[2048,256]{1,0:T(8,128)(2,1)S(1)} %get-tuple-element.12.ol_ref, ...), custom_call_target="tpu_custom_call" | custom-call | tf_op jit(solution)/shard_map/finish/pallas_call | solution.py:372
  253.4 0.0 copy-done.1
  253.4 1.8 copy.10
Async XLA Ops:
  53.9 33.6 %copy-start = (f32[4,2,256,256]{3,2,1,0:T(8,128)}, f32[4,2,256,256]{3,2,1,0:T(8,128)S(1)}, u32[]{:S(2)}) copy-start(f32[4,2,256,256]{3,2,1,0:T(8,128)S(1)} %left_sum.1) | copy-start | bytes 6291460
  214.4 39.0 %copy-start.1 = (f32[3584,256]{1,0:T(8,128)S(1)}, f32[3584,256]{1,0:T(8,128)}, u32[]{:S(2)}) copy-start(f32[3584,256]{1,0:T(8,128)} %get-tuple-element.23) | copy-start | bytes 11010052

commit v2 on v1

v2 whole, which is shorter than its diff:
```python
import functools
import jax
import jax.numpy as jnp
from jax import lax
from jax.experimental import pallas as pl
from jax.experimental.pallas import tpu as pltpu
from jax.sharding import PartitionSpec as P

HI = lax.Precision.HIGHEST
MESH = pl.DeviceIdType.MESH
F32, BF16 = jnp.float32, jnp.bfloat16
CHUNK = 128
PANEL = 16


def rcopy(src, dst, ssem, rsem, device):
    return pltpu.make_async_remote_copy(
        src_ref=src, dst_ref=dst, send_sem=ssem, recv_sem=rsem, device_id=device, device_id_type=MESH
    )


def signal(sem, device):
    pl.semaphore_signal(sem, inc=1, device_id=device, device_id_type=MESH)


def split(a):
    hi = a.astype(BF16)
    return hi, (a - hi.astype(F32)).astype(BF16)


def dot(a, b):
    return jnp.dot(a, b, preferred_element_type=F32)


def dot3(ah, al, bh, bl):
    return dot(ah, bh) + (dot(ah, bl) + dot(al, bh))


def left_sum(chips, fused, *refs):
    if fused:
        m_ref, g_ref, rp_ref, o_ref, x, rh, rl, mbuf, gbuf, sf, *refs = refs
    else:
        x, o_ref, *refs = refs
    got, acc, sums, full, s1, r1, s2, r2, s3, r3, s4, r4 = refs
    me = lax.axis_index("col")
    core, chip = lax.rem(me, 2), me // 2
    sib = {"col": me + 1 - 2 * core}
    s = acc.shape[1]

    def place(i):
        k = lax.rem(lax.rem(i, chips) + 1, chips)
        return k, lax.rem(chip + k, chips), jnp.where(i < chips, 1 - core, core)

    def fetch(i):
        _, q, c = place(i)
        rows = pl.ds(pl.multiple_of((2 * q + c) * s, s), s)
        slot = lax.rem(i, 2)
        return (
            pltpu.make_async_copy(m_ref.at[rows], mbuf.at[slot], sf.at[0, slot]),
            pltpu.make_async_copy(g_ref.at[rows], gbuf.at[slot], sf.at[1, slot]),
        )

    if fused:
        for f in fetch(0):
            f.start()
    barrier = pltpu.get_barrier_semaphore()
    signal(barrier, sib)
    for k in range(1, chips):
        signal(barrier, {"col": 2 * lax.rem(chip + k, chips) + core})
    if fused:
        hi, lo = split(rp_ref[...])
        rh[...] = hi
        rl[...] = lo
    pl.semaphore_wait(barrier, chips)

    def pair(k):
        q = lax.rem(chip + k, chips)
        return rcopy(x.at[q, 1 - core], got.at[k], s1.at[k], r1.at[k], sib)

    def scatter(k):
        q = lax.rem(chip + k, chips)
        return rcopy(acc.at[k], sums.at[k], s2.at[k], r2.at[k], {"col": 2 * q + core})

    def turn(i, carry):
        k, q, c = place(i)
        if fused:
            @pl.when(i + 1 < 2 * chips)
            def _():
                for f in fetch(i + 1):
                    f.start()

            for f in fetch(i):
                f.wait()
            slot = lax.rem(i, 2)
            depth = rh.shape[0]
            step = divisor(depth, 512)
            total = jnp.zeros((s, rh.shape[1]), F32)
            for at in range(0, depth, step):
                here = pl.ds(at, step)
                hi, lo = split(mbuf[slot, :, here] + gbuf[slot, :, here].astype(F32))
                total = total + dot3(hi, lo, rh[here, :], rl[here, :])
            x[q, c] = total

        @pl.when(i < chips)
        def _():
            pair(k).start()

        @pl.when(i >= chips)
        def _():
            pair(k).wait_recv()
            acc[k] = x[q, core] + got[k]

            @pl.when(k > 0)
            def _():
                scatter(k).start()

        return carry

    lax.fori_loop(0, 2 * chips, turn, 0)
    total = acc[0]
    for k in range(1, chips):
        scatter(k).wait_recv()
        total = total + sums[k]
    full[chip, core] = total

    def gather(k):
        q = lax.rem(chip + k, chips)
        return rcopy(full.at[chip, core], full.at[chip, core], s3.at[k], r3.at[k], {"col": 2 * q + core})

    def forward(k):
        q = lax.rem(chip - k + chips, chips)
        return rcopy(full.at[q, core], full.at[q, core], s4.at[k], r4.at[k], sib)

    for k in range(1, chips):
        gather(k).start()
    forward(0).start()
    for k in range(1, chips):
        q = lax.rem(chip - k + chips, chips)
        rcopy(full.at[q, core], full.at[q, core], s3.at[k], r3.at[k], {"col": 2 * q + core}).wait_recv()
        forward(k).start()
    for k in range(chips):
        q = lax.rem(chip - k + chips, chips)
        rcopy(full.at[q, 1 - core], full.at[q, 1 - core], s4.at[k], r4.at[k], sib).wait_recv()
    for k in range(chips):
        pair(k).wait_send()
        forward(k).wait_send()
        if k:
            scatter(k).wait_send()
            gather(k).wait_send()
    o_ref[...] = full[...]


def left_factor(momentum, gradient, right_prev, n):
    rows, ffl = momentum.shape
    rank = right_prev.shape[1]
    chips, s = n // 2, rows // n
    fused = s % 16 == 0
    dma = pltpu.SemaphoreType.DMA
    vm = pl.BlockSpec(memory_space=pltpu.VMEM)
    hbm = pl.BlockSpec(memory_space=pl.ANY)
    if fused:
        args, specs = (momentum, gradient, right_prev), [hbm, hbm, vm]
        extra = [
            pltpu.VMEM((chips, 2, s, rank), F32),
            pltpu.VMEM((ffl, rank), BF16),
            pltpu.VMEM((ffl, rank), BF16),
            pltpu.VMEM((2, s, ffl), F32),
            pltpu.VMEM((2, s, ffl), BF16),
            dma((2, 2)),
        ]
    else:
        merged = momentum + gradient.astype(F32)
        part = jnp.dot(merged, right_prev, precision=lax.Precision.HIGH, preferred_element_type=F32)
        args, specs, extra = (part.reshape(chips, 2, s, rank),), [vm], []
    out = pl.pallas_call(
        functools.partial(left_sum, chips, fused),
        out_shape=jax.ShapeDtypeStruct((chips, 2, s, rank), F32),
        in_specs=specs,
        out_specs=vm,
        scratch_shapes=extra
        + [pltpu.VMEM((chips, s, rank), F32)] * 3
        + [pltpu.VMEM((chips, 2, s, rank), F32)]
        + [dma((chips,))] * 8,
        compiler_params=pltpu.CompilerParams(
            collective_id=0, has_side_effects=True, vmem_limit_bytes=48 * 2**20
        ),
        name="left_sum",
    )(*args)
    return out.reshape(rows, rank)


def panel_step(mat, p):
    rank, wide = mat.shape
    first = p * PANEL
    rows0 = pl.ds(pl.multiple_of(first, PANEL), PANEL)
    rows = mat[rows0, :]
    pick = lax.broadcasted_iota(jnp.int32, (rank, 128), 0) == first + lax.broadcasted_iota(
        jnp.int32, (rank, 128), 1
    )
    block = jnp.dot(rows[:, :rank], pick.astype(F32), precision=HI, preferred_element_type=F32)
    sub = lax.broadcasted_iota(jnp.int32, (PANEL, 128), 0)
    lane = lax.broadcasted_iota(jnp.int32, (PANEL, 128), 1)
    block = jnp.where(lane < PANEL, block, jnp.where(lane - PANEL == sub, 1.0, 0.0))
    for k in range(PANEL):
        col = jnp.broadcast_to(block[:, k : k + 1], (PANEL, 128))
        pivot = jnp.broadcast_to(col[k : k + 1, :], (PANEL, 128))
        inv = lax.rsqrt(pivot)
        inv = inv * (1.5 - 0.5 * (pivot * inv) * inv)
        u = jnp.broadcast_to(block[k : k + 1, :], (PANEL, 128)) * inv
        factor = jnp.where(sub > k, col * inv, 0.0)
        block = jnp.where(sub == k, u, block - factor * u)
    u = jnp.dot(block[:, PANEL : 2 * PANEL], rows, precision=HI, preferred_element_type=F32)
    mat[rows0, :] = u
    drop = lax.dot_general(
        u[:, :rank], u, (((0,), (0,)), ((), ())), precision=HI, preferred_element_type=F32
    )
    below = lax.broadcasted_iota(jnp.int32, (rank, wide), 0) >= first + PANEL
    mat[...] = jnp.where(below, mat[...] - drop, mat[...])


def times_inverse(a, inverse):
    return lax.dot_general(
        a, inverse, (((1,), (1,)), ((), ())), precision=HI, preferred_element_type=F32
    )


def right_sum(
    n, cols, ff, m_ref, g_ref, left_ref,
    next_ref, nh_ref, nl_ref, rb_ref, oh_ref, ol_ref,
    x, outer_in, inner_in, mat, colsq, lh, ll, mbuf, gbuf, sf, s_in, r_outer, s_out, r_inner, s_c, r_c,
):
    me, mc = lax.axis_index("row"), lax.axis_index("col")
    half = n // 2
    low = me < half
    depth = jnp.where(low, half - 1 - me, me - half)
    inward = {"row": jnp.where(low, me + 1, me - 1)}
    has_outer = depth < half - 1
    outward = {"row": jnp.where(has_outer, jnp.where(low, me - 1, me + 1), me)}
    rows, rank = left_ref.shape
    ffl = m_ref.shape[1]
    chunks = (rank + ffl) // CHUNK
    gram_chunks, panels = rank // CHUNK, rank // PANEL
    spread = max(chunks - gram_chunks, panels)

    def fetch(w):
        here = pl.ds(pl.multiple_of(w * CHUNK, CHUNK), CHUNK)
        slot = lax.rem(w, 2)
        return (
            pltpu.make_async_copy(m_ref.at[:, here], mbuf.at[slot], sf.at[0, slot]),
            pltpu.make_async_copy(g_ref.at[:, here], gbuf.at[slot], sf.at[1, slot]),
        )

    for f in fetch(0):
        f.start()

    barrier = pltpu.get_barrier_semaphore()
    for k in range(1, cols):
        signal(barrier, {"col": lax.rem(mc + k, cols)})
    signal(barrier, inward)

    @pl.when(has_outer)
    def _():
        signal(barrier, outward)

    for b in range(0, rows, CHUNK):
        hi, lo = split(left_ref[pl.ds(b, CHUNK), :].T)
        lh[:, pl.ds(b, CHUNK)] = hi
        ll[:, pl.ds(b, CHUNK)] = lo
    gram = lax.dot_general(
        left_ref[...], left_ref[...], (((0,), (0,)), ((), ())), precision=HI, preferred_element_type=F32
    )
    for c in range(gram_chunks):
        x[c] = gram[:, c * CHUNK : (c + 1) * CHUNK]

    @pl.when(has_outer)
    def _():
        pl.semaphore_wait(barrier, cols + 1)

    @pl.when(jnp.logical_not(has_outer))
    def _():
        pl.semaphore_wait(barrier, cols)

    def to_inner(c):
        return rcopy(x.at[c], outer_in.at[c], s_in.at[c], r_outer.at[c], inward)

    def to_partner(c):
        return rcopy(x.at[c], inner_in.at[c], s_in.at[c], r_inner.at[c], inward)

    def to_outer(c):
        return rcopy(outer_in.at[c], inner_in.at[c], s_out.at[c], r_inner.at[c], outward)

    lag = 2 + 3 * depth

    def turn(t, carry):
        @pl.when((t >= gram_chunks) & (t < chunks))
        def _():
            w = t - gram_chunks

            @pl.when(w + 1 < chunks - gram_chunks)
            def _():
                for f in fetch(w + 1):
                    f.start()

            for f in fetch(w):
                f.wait()
            slot = lax.rem(w, 2)
            step = divisor(rows, 512)
            total = jnp.zeros((rank, CHUNK), F32)
            for b in range(0, rows, step):
                here = pl.ds(b, step)
                hi, lo = split(mbuf[slot, here, :] + gbuf[slot, here, :].astype(F32))
                total = total + dot3(lh[:, here], ll[:, here], hi, lo)
            x[t] = total

        @pl.when(t < chunks)
        def _():
            @pl.when(has_outer)
            def _():
                to_inner(t).wait_recv()
                x[t] = x[t] + outer_in[t]

            @pl.when(depth > 0)
            def _():
                to_inner(t).start()

            @pl.when(depth == 0)
            def _():
                to_partner(t).start()

        c = t - lag

        @pl.when((c >= 0) & (c < chunks))
        def _():
            to_partner(c).wait_recv()

            @pl.when(depth == 0)
            def _():
                outer_in[c] = x[c] + inner_in[c]

            @pl.when(depth > 0)
            def _():
                outer_in[c] = inner_in[c]

            @pl.when(has_outer)
            def _():
                to_outer(c).start()

        @pl.when(c == gram_chunks - 1)
        def _():
            for b in range(gram_chunks):
                mat[:, pl.ds(b * CHUNK, CHUNK)] = outer_in[b]
            i0 = lax.broadcasted_iota(jnp.int32, (rank, rank), 0)
            i1 = lax.broadcasted_iota(jnp.int32, (rank, rank), 1)
            mat[:, pl.ds(rank, rank)] = jnp.where(i0 == i1, 1.0, 0.0).astype(F32)

        at = jnp.maximum(c - gram_chunks, 0)
        p = at * panels // spread

        @pl.when((c >= gram_chunks) & (c < gram_chunks + spread) & ((at + 1) * panels // spread > p))
        def _():
            panel_step(mat, p)

        return carry

    turns = gram_chunks + spread + 2 + 3 * (half - 1)
    lax.fori_loop(0, turns, turn, 0)

    inverse = mat[:, pl.ds(rank, rank)]

    def to_right(b, total):
        here = pl.ds(pl.multiple_of(b * CHUNK, CHUNK), CHUNK)
        c = b + gram_chunks
        value = jnp.dot(inverse, outer_in[c], precision=HI, preferred_element_type=F32)
        inner_in[c] = value
        rb_ref[:, here] = (0.05 * value).astype(BF16)
        return total + value * value

    part = lax.fori_loop(0, ffl // CHUNK, to_right, jnp.zeros((rank, CHUNK), F32))
    colsq[mc] = jnp.broadcast_to(jnp.sum(part.T, axis=0, keepdims=True), (8, rank))

    def share(k):
        return rcopy(
            colsq.at[mc], colsq.at[mc], s_c.at[k - 1], r_c.at[k - 1], {"col": lax.rem(mc + k, cols)}
        )

    for k in range(1, cols):
        share(k).start()

    def to_ortho(b, carry):
        here = pl.ds(pl.multiple_of(b * CHUNK, CHUNK), CHUNK)
        hi, lo = split(times_inverse(left_ref[here, :], inverse))
        oh_ref[here, :] = hi
        ol_ref[here, :] = lo
        return carry

    lax.fori_loop(0, left_ref.shape[0] // CHUNK, to_ortho, 0)

    for k in range(1, cols):
        q = lax.rem(mc - k + cols, cols)
        rcopy(colsq.at[q], colsq.at[q], s_c.at[k - 1], r_c.at[k - 1], {"col": q}).wait_recv()
    total = colsq[0]
    for q in range(1, cols):
        total = total + colsq[q]
    scale = jnp.broadcast_to(1.0 / jnp.sqrt(total[:1] / ff + 1e-6), (CHUNK, rank)).T

    def to_next(b, carry):
        here = pl.ds(pl.multiple_of(b * CHUNK, CHUNK), CHUNK)
        value = inner_in[b + gram_chunks] * scale
        next_ref[here, :] = value.T
        hi, lo = split(value)
        nh_ref[:, here] = hi
        nl_ref[:, here] = lo
        return carry

    lax.fori_loop(0, ffl // CHUNK, to_next, 0)

    def drain(c, carry):
        to_inner(c).wait_send()

        @pl.when(has_outer)
        def _():
            to_outer(c).wait_send()

        return carry

    lax.fori_loop(0, chunks, drain, 0)
    for k in range(1, cols):
        share(k).wait_send()


def right_factor(momentum, gradient, left, n, cols, ff):
    (rows, rank), ffl = left.shape, momentum.shape[1]
    chunks = (rank + ffl) // CHUNK
    dma = pltpu.SemaphoreType.DMA
    vm = pl.BlockSpec(memory_space=pltpu.VMEM)
    hbm = pl.BlockSpec(memory_space=pl.ANY)
    return pl.pallas_call(
        functools.partial(right_sum, n, cols, float(ff)),
        out_shape=[jax.ShapeDtypeStruct((ffl, rank), F32)]
        + [jax.ShapeDtypeStruct((rank, ffl), BF16)] * 3
        + [jax.ShapeDtypeStruct((rows, rank), BF16)] * 2,
        in_specs=[hbm, hbm, vm],
        out_specs=[vm] * 6,
        scratch_shapes=[pltpu.VMEM((chunks, rank, CHUNK), F32)] * 3
        + [
            pltpu.VMEM((rank, 2 * rank), F32),
            pltpu.VMEM((cols, 8, rank), F32),
            pltpu.VMEM((rank, rows), BF16),
            pltpu.VMEM((rank, rows), BF16),
            pltpu.VMEM((2, rows, CHUNK), F32),
            pltpu.VMEM((2, rows, CHUNK), BF16),
            dma((2, 2)),
        ]
        + [dma((chunks,))] * 4
        + [dma((cols - 1,))] * 2,
        compiler_params=pltpu.CompilerParams(
            collective_id=1, has_side_effects=True, vmem_limit_bytes=48 * 2**20
        ),
        name="right_sum",
    )(momentum, gradient, left)


def finish(factor, m_ref, g_ref, oh_ref, ol_ref, nh_ref, nl_ref, rb_ref, new_ref, up_ref):
    oh, nh = oh_ref[...], nh_ref[...]
    new_ref[...] = (m_ref[...] + g_ref[...].astype(F32)) - dot(oh, rb_ref[...])
    up = dot(
        jnp.concatenate([oh, oh, ol_ref[...]], axis=1), jnp.concatenate([nh, nl_ref[...], nh], axis=0)
    )
    up_ref[...] = (factor * up).astype(BF16)


def divisor(size, most):
    return max(t for t in range(128, most + 1, 128) if size % t == 0)


def outputs(m, g, oh, ol, nh, nl, rb, factor):
    rows, cols = m.shape
    rank = oh.shape[1]
    tm, tn = divisor(rows, 256), divisor(cols, 1792)
    tile = pl.BlockSpec((tm, tn), lambda j, i: (i, j))
    o = pl.BlockSpec((tm, rank), lambda j, i: (i, 0))
    r = pl.BlockSpec((rank, tn), lambda j, i: (0, j))
    return pl.pallas_call(
        functools.partial(finish, factor),
        grid=(cols // tn, rows // tm),
        out_shape=[jax.ShapeDtypeStruct((rows, cols), F32), jax.ShapeDtypeStruct((rows, cols), BF16)],
        in_specs=[tile, tile, o, o, r, r, r],
        out_specs=[tile, tile],
        compiler_params=pltpu.CompilerParams(vmem_limit_bytes=48 * 2**20),
        name="finish",
    )(m, g, oh, ol, nh, nl, rb)


def solution(mesh):
    n, cols = mesh.shape["row"], mesh.shape["col"]

    def on_device(momentum, gradient, right_prev):
        ff, rank = right_prev.shape[0] * cols, right_prev.shape[1]
        d = momentum.shape[0] * n
        left = left_factor(momentum, gradient, right_prev, cols)
        right_next, nh, nl, rb, oh, ol = right_factor(momentum, gradient, left, n, cols, ff)
        new_momentum, update = outputs(
            momentum, gradient, oh, ol, nh, nl, rb, (d / rank) ** 0.5
        )
        return new_momentum, right_next, update

    in_specs = (P("row", "col"), P("row", "col"), P("col", None))
    out_specs = (P("row", "col"), P("col", None), P("row", "col"))
    return jax.shard_map(
        on_device, mesh=mesh, in_specs=in_specs, out_specs=out_specs, check_vma=False
    )
```

time: 256 us -> 230 us (0.90)
  matrix products: 53.5 us -> 0 us
  Pallas kernels: 199 us -> 223 us
  local copies, waits for them, and re-layouts: 1.85 us -> 5.19 us
    dot_general x3 -> x0, matrix products: 53.5 us -> none  [the longest x1 29.9 us: on_device(): jnp.dot(merged.T, left, precision=lax.Precision.HIGH, preferred_element_t...]
    pallas_call x1, Pallas kernels: 127 us -> 141 us  [right_factor(): pl.pallas_call(functools.partial(right_sum, n, cols, float(ff)), out_shap...]
    pallas_call x1, Pallas kernels: 33.3 us -> 44.2 us  [left_factor(): pl.pallas_call(functools.partial(left_sum, chips, fused), out_shape=jax.S...]
    unnamed x5 -> x7, local copies, waits for them, and re-layouts: 1.85 us -> 5.19 us
where the time goes in v2:
time: 230 us; the launch traced here: 229 us
  Pallas kernels  223 us (97%)
  local copies, waits for them, and re-layouts  5.19 us (2%)
    pallas_call x1, Pallas kernels, right_factor(): pl.pallas_call(functools.partial(right_sum, n, cols, float(ff)), out_shap...  141 us
    pallas_call x1, Pallas kernels, left_factor(): pl.pallas_call(functools.partial(left_sum, chips, fused), out_shape=jax.S...  44.2 us
    pallas_call x1, Pallas kernels, outputs(): pl.pallas_call(functools.partial(finish, factor), grid=(cols // tn, rows...  38.3 us
    unnamed x7, local copies, waits for them, and re-layouts  5.19 us

profile of v2, /device:TPU:0, one launch (start us, length us, event | category | flops | bytes accessed | tf_op | source)
XLA Modules:
  0.0 229.0 jit_solution(17528568469339441769)
XLA Ops:
  0.6 0.0 copy-start.1
  0.6 2.0 copy-done.1
  2.7 44.2 %left_sum.1 = f32[4,2,256,256]{3,2,1,0:T(8,128)S(1)} custom-call(f32[2048,3584]{1,0:T(8,128)} %m_ref.3, bf16[2048,3584]{1,0:T(8,128)(2,1)} %g_ref.3, f32[3584,256]{1,0:T(8,128)S(1)} %copy-done.1), custom_call_target="tpu_custom_call" | custom-call | tf_op jit(solution)/shard_map/left_sum/pallas_call | solution.py:175
  46.8 0.0 copy-start
  46.9 1.3 copy-done
  48.2 140.7 %right_sum.1 = (f32[3584,256]{1,0:T(8,128)}, bf16[256,3584]{1,0:T(8,128)(2,1)S(1)}, bf16[256,3584]{1,0:T(8,128)(2,1)S(1)}, bf16[256,3584]{1,0:T(8,128)(2,1)}, bf...) custom-call(f32[2048,3584]{1,0:T(8,128)} %m_ref.3, bf16[2048,3584]{1,0:T(8,128)(2,1)} %g_ref.3, f32[2048,256]{1,0:T(8,128)} %bitcast.1), custom_call_target="tpu_custom_call" | custom-call | tf_op jit(solution)/shard_map/right_sum/pallas_call | solution.py:437
  188.8 0.0 copy-start.2
  188.9 38.3 %finish.1 = (f32[2048,3584]{1,0:T(8,128)}, bf16[2048,3584]{1,0:T(8,128)(2,1)}) custom-call(f32[2048,3584]{1,0:T(8,128)} %m_ref.3, bf16[2048,3584]{1,0:T(8,128)(2,1)} %g_ref.3, bf16[2048,256]{1,0:T(8,128)(2,1)S(1)} %get-tuple-element.11.oh_ref, bf16[2048,256]{1,0:T(8,128)(2,1)S(1)} %get-tuple-element.12.ol_ref, ...), custom_call_target="tpu_custom_call" | custom-call | tf_op jit(solution)/shard_map/finish/pallas_call | solution.py:483
  227.2 0.0 copy-done.2
  227.2 1.8 copy.7
Async XLA Ops:
  0.6 2.0 copy-start.1
  46.8 1.3 copy-start
  188.8 38.3 %copy-start.2 = (f32[3584,256]{1,0:T(8,128)S(1)}, f32[3584,256]{1,0:T(8,128)}, u32[]{:S(2)}) copy-start(f32[3584,256]{1,0:T(8,128)} %get-tuple-element.23) | copy-start | bytes 11010052

commit v3 on v2

--- a/solution.py
+++ b/solution.py
@@ -10,7 +10,7 @@
 MESH = pl.DeviceIdType.MESH
 F32, BF16 = jnp.float32, jnp.bfloat16
 CHUNK = 128
-PANEL = 16
+PANEL = 32
 
 
 def rcopy(src, dst, ssem, rsem, device):
@@ -367,6 +367,16 @@
 
     inverse = mat[:, pl.ds(rank, rank)]
 
+    def blocks(count, body, carry):
+        group = max(g for g in (1, 2, 4) if count % g == 0)
+
+        def several(b, carry):
+            for g in range(group):
+                carry = body(b * group + g, carry)
+            return carry
+
+        return lax.fori_loop(0, count // group, several, carry)
+
     def to_right(b, total):
         here = pl.ds(pl.multiple_of(b * CHUNK, CHUNK), CHUNK)
         c = b + gram_chunks
@@ -375,7 +385,7 @@
         rb_ref[:, here] = (0.05 * value).astype(BF16)
         return total + value * value
 
-    part = lax.fori_loop(0, ffl // CHUNK, to_right, jnp.zeros((rank, CHUNK), F32))
+    part = blocks(ffl // CHUNK, to_right, jnp.zeros((rank, CHUNK), F32))
     colsq[mc] = jnp.broadcast_to(jnp.sum(part.T, axis=0, keepdims=True), (8, rank))
 
     def share(k):
@@ -393,7 +403,7 @@
         ol_ref[here, :] = lo
         return carry
 
-    lax.fori_loop(0, left_ref.shape[0] // CHUNK, to_ortho, 0)
+    blocks(rows // CHUNK, to_ortho, 0)
 
     for k in range(1, cols):
         q = lax.rem(mc - k + cols, cols)
@@ -412,7 +422,7 @@
         nl_ref[:, here] = lo
         return carry
 
-    lax.fori_loop(0, ffl // CHUNK, to_next, 0)
+    blocks(ffl // CHUNK, to_next, 0)
 
     def drain(c, carry):
         to_inner(c).wait_send()
@@ -476,7 +486,7 @@
 def outputs(m, g, oh, ol, nh, nl, rb, factor):
     rows, cols = m.shape
     rank = oh.shape[1]
-    tm, tn = divisor(rows, 256), divisor(cols, 1792)
+    tm, tn = divisor(rows, 2048), divisor(cols, 256)
     tile = pl.BlockSpec((tm, tn), lambda j, i: (i, j))
     o = pl.BlockSpec((tm, rank), lambda j, i: (i, 0))
     r = pl.BlockSpec((rank, tn), lambda j, i: (0, j))

time: 230 us -> 231 us (level)
    pallas_call x1, Pallas kernels: 141 us -> 146 us  [right_factor(): pl.pallas_call(functools.partial(right_sum, n, cols, float(ff)), out_shap...]
    pallas_call x1, Pallas kernels: 38.3 us -> 34.9 us  [outputs(): pl.pallas_call(functools.partial(finish, factor), grid=(cols // tn, rows...]
where the time goes in v3:
time: 231 us
  Pallas kernels  225 us (97%)
  local copies, waits for them, and re-layouts  5.19 us (2%)
    pallas_call x1, Pallas kernels, right_factor(): pl.pallas_call(functools.partial(right_sum, n, cols, float(ff)), out_shap...  146 us
    pallas_call x1, Pallas kernels, left_factor(): pl.pallas_call(functools.partial(left_sum, chips, fused), out_shape=jax.S...  44.2 us
    pallas_call x1, Pallas kernels, outputs(): pl.pallas_call(functools.partial(finish, factor), grid=(cols // tn, rows...  34.9 us
    unnamed x7, local copies, waits for them, and re-layouts  5.19 us

profile of v3, /device:TPU:0, one launch (start us, length us, event | category | flops | bytes accessed | tf_op | source)
XLA Modules:
  0.0 231.0 jit_solution(183546014335151176)
XLA Ops:
  0.6 0.0 copy-start.1
  0.6 2.0 copy-done.1
  2.7 44.2 %left_sum.1 = f32[4,2,256,256]{3,2,1,0:T(8,128)S(1)} custom-call(f32[2048,3584]{1,0:T(8,128)} %m_ref.3, bf16[2048,3584]{1,0:T(8,128)(2,1)} %g_ref.3, f32[3584,256]{1,0:T(8,128)S(1)} %copy-done.1), custom_call_target="tpu_custom_call" | custom-call | tf_op jit(solution)/shard_map/left_sum/pallas_call | solution.py:175
  46.8 0.0 copy-start
  46.9 1.3 copy-done
  48.2 146.1 %right_sum.1 = (f32[3584,256]{1,0:T(8,128)}, bf16[256,3584]{1,0:T(8,128)(2,1)S(1)}, bf16[256,3584]{1,0:T(8,128)(2,1)S(1)}, bf16[256,3584]{1,0:T(8,128)(2,1)}, bf...) custom-call(f32[2048,3584]{1,0:T(8,128)} %m_ref.3, bf16[2048,3584]{1,0:T(8,128)(2,1)} %g_ref.3, f32[2048,256]{1,0:T(8,128)} %bitcast.1), custom_call_target="tpu_custom_call" | custom-call | tf_op jit(solution)/shard_map/right_sum/pallas_call | solution.py:447
  194.2 0.0 copy-start.2
  194.3 34.9 %finish.1 = (f32[2048,3584]{1,0:T(8,128)}, bf16[2048,3584]{1,0:T(8,128)(2,1)}) custom-call(f32[2048,3584]{1,0:T(8,128)} %m_ref.3, bf16[2048,3584]{1,0:T(8,128)(2,1)} %g_ref.3, bf16[2048,256]{1,0:T(8,128)(2,1)S(1)} %get-tuple-element.11.oh_ref, bf16[2048,256]{1,0:T(8,128)(2,1)S(1)} %get-tuple-element.12.ol_ref, ...), custom_call_target="tpu_custom_call" | custom-call | tf_op jit(solution)/shard_map/finish/pallas_call | solution.py:493
  229.1 0.0 copy-done.2
  229.1 1.8 copy.7
Async XLA Ops:
  0.6 2.0 copy-start.1
  46.8 1.3 copy-start
  194.2 34.9 %copy-start.2 = (f32[3584,256]{1,0:T(8,128)S(1)}, f32[3584,256]{1,0:T(8,128)}, u32[]{:S(2)}) copy-start(f32[3584,256]{1,0:T(8,128)} %get-tuple-element.23) | copy-start | bytes 11010052

commit v4 on v3

--- a/solution.py
+++ b/solution.py
@@ -10,7 +10,7 @@
 MESH = pl.DeviceIdType.MESH
 F32, BF16 = jnp.float32, jnp.bfloat16
 CHUNK = 128
-PANEL = 32
+PANEL = 16
 
 
 def rcopy(src, dst, ssem, rsem, device):
@@ -292,7 +292,13 @@
     lag = 2 + 3 * depth
 
     def turn(t, carry):
-        @pl.when((t >= gram_chunks) & (t < chunks))
+        c = t - lag
+        at = jnp.maximum(c - gram_chunks, 0)
+        p = at * panels // spread
+        product = (t >= gram_chunks) & (t < chunks)
+        panel = (c >= gram_chunks) & (c < gram_chunks + spread) & ((at + 1) * panels // spread > p)
+
+        @pl.when(product)
         def _():
             w = t - gram_chunks
 
@@ -303,7 +309,9 @@
 
             for f in fetch(w):
                 f.wait()
-            slot = lax.rem(w, 2)
+
+        def multiply():
+            slot = lax.rem(jnp.maximum(t - gram_chunks, 0), 2)
             step = divisor(rows, 512)
             total = jnp.zeros((rank, CHUNK), F32)
             for b in range(0, rows, step):
@@ -312,6 +320,19 @@
                 total = total + dot3(lh[:, here], ll[:, here], hi, lo)
             x[t] = total
 
+        @pl.when(product & panel)
+        def _():
+            multiply()
+            panel_step(mat, p)
+
+        @pl.when(product & jnp.logical_not(panel))
+        def _():
+            multiply()
+
+        @pl.when(panel & jnp.logical_not(product))
+        def _():
+            panel_step(mat, p)
+
         @pl.when(t < chunks)
         def _():
             @pl.when(has_outer)
@@ -326,8 +347,6 @@
             @pl.when(depth == 0)
             def _():
                 to_partner(t).start()
-
-        c = t - lag
 
         @pl.when((c >= 0) & (c < chunks))
         def _():
@@ -352,13 +371,6 @@
             i0 = lax.broadcasted_iota(jnp.int32, (rank, rank), 0)
             i1 = lax.broadcasted_iota(jnp.int32, (rank, rank), 1)
             mat[:, pl.ds(rank, rank)] = jnp.where(i0 == i1, 1.0, 0.0).astype(F32)
-
-        at = jnp.maximum(c - gram_chunks, 0)
-        p = at * panels // spread
-
-        @pl.when((c >= gram_chunks) & (c < gram_chunks + spread) & ((at + 1) * panels // spread > p))
-        def _():
-            panel_step(mat, p)
 
         return carry
 

time: 231 us -> 218 us (0.944)
  Pallas kernels: 225 us -> 212 us
    pallas_call x1, Pallas kernels: 146 us -> 133 us  [right_factor(): pl.pallas_call(functools.partial(right_sum, n, cols, float(ff)), out_shap...]
where the time goes in v4:
time: 218 us
  Pallas kernels  212 us (97%)
  local copies, waits for them, and re-layouts  5.19 us (2%)
    pallas_call x1, Pallas kernels, right_factor(): pl.pallas_call(functools.partial(right_sum, n, cols, float(ff)), out_shap...  133 us
    pallas_call x1, Pallas kernels, left_factor(): pl.pallas_call(functools.partial(left_sum, chips, fused), out_shape=jax.S...  44.2 us
    pallas_call x1, Pallas kernels, outputs(): pl.pallas_call(functools.partial(finish, factor), grid=(cols // tn, rows...  34.9 us
    unnamed x7, local copies, waits for them, and re-layouts  5.19 us

profile of v4, /device:TPU:0, one launch (start us, length us, event | category | flops | bytes accessed | tf_op | source)
XLA Modules:
  0.0 217.5 jit_solution(17592044095351479989)
XLA Ops:
  0.6 0.0 copy-start.1
  0.6 2.0 copy-done.1
  2.7 44.2 %left_sum.1 = f32[4,2,256,256]{3,2,1,0:T(8,128)S(1)} custom-call(f32[2048,3584]{1,0:T(8,128)} %m_ref.3, bf16[2048,3584]{1,0:T(8,128)(2,1)} %g_ref.3, f32[3584,256]{1,0:T(8,128)S(1)} %copy-done.1), custom_call_target="tpu_custom_call" | custom-call | tf_op jit(solution)/shard_map/left_sum/pallas_call | solution.py:175
  46.8 0.0 copy-start
  46.9 1.3 copy-done
  48.2 132.6 %right_sum.1 = (f32[3584,256]{1,0:T(8,128)}, bf16[256,3584]{1,0:T(8,128)(2,1)S(1)}, bf16[256,3584]{1,0:T(8,128)(2,1)S(1)}, bf16[256,3584]{1,0:T(8,128)(2,1)}, bf...) custom-call(f32[2048,3584]{1,0:T(8,128)} %m_ref.3, bf16[2048,3584]{1,0:T(8,128)(2,1)} %g_ref.3, f32[2048,256]{1,0:T(8,128)} %bitcast.1), custom_call_target="tpu_custom_call" | custom-call | tf_op jit(solution)/shard_map/right_sum/pallas_call | solution.py:459
  180.8 0.0 copy-start.2
  180.8 34.9 %finish.1 = (f32[2048,3584]{1,0:T(8,128)}, bf16[2048,3584]{1,0:T(8,128)(2,1)}) custom-call(f32[2048,3584]{1,0:T(8,128)} %m_ref.3, bf16[2048,3584]{1,0:T(8,128)(2,1)} %g_ref.3, bf16[2048,256]{1,0:T(8,128)(2,1)S(1)} %get-tuple-element.11.oh_ref, bf16[2048,256]{1,0:T(8,128)(2,1)S(1)} %get-tuple-element.12.ol_ref, ...), custom_call_target="tpu_custom_call" | custom-call | tf_op jit(solution)/shard_map/finish/pallas_call | solution.py:505
  215.7 0.0 copy-done.2
  215.7 1.8 copy.7
Async XLA Ops:
  0.6 2.0 copy-start.1
  46.8 1.3 copy-start
  180.8 34.9 %copy-start.2 = (f32[3584,256]{1,0:T(8,128)S(1)}, f32[3584,256]{1,0:T(8,128)}, u32[]{:S(2)}) copy-start(f32[3584,256]{1,0:T(8,128)} %get-tuple-element.23) | copy-start | bytes 11010052
